TPU v7x, 128 devices: a whole 4x4x4 slice. The times are simulated.
128 devices in a mesh: aux: 16 (over x, z), orb: 8 (over y, core).
Axes of the slice: x: 4, y: 4, z: 4, core: 2. Of those that a mesh axis runs over, the one named last changes fastest.
Arguments:
- integrals: bfloat16 [32, 128, 8, 128, 128], P('aux', 'orb'), may hold values from -0.1875 to 0.1875
- panels: bfloat16 [8, 128, 1920], P('orb'), may hold values from -6 to 6
- screen: int32 [16, 128, 8], replicated, may hold values from 0 to 1, as said below
- owner_map: int32 [8], replicated, may hold values from 0 to 7, each once
Outputs:
- halves: bfloat16 [128, 32, 128, 1920], P(('orb', 'aux'))
- kblocks: float32 [128, 128, 128], P(('orb', 'aux'))
Inputs may be any that keep to these rules, and one draw needn't show every extreme that they name: `screen`: 1 where the block of an auxiliary tile, an orbital row block and a panel survives screening, 0 where it is screened out; the kept share differs from row block to row block. A permutation: panel j is stored at position owner_map[j] of panels.
All inputs are finite; a program needn't handle non-finite values.
Results may differ from a plain program's by a relative error of at most 0.001.
Values may be sent and summed in bfloat16 or wider, within the bound.
A program may use at most 128 MiB of HBM per device.

v0:
```python
import jax
import jax.numpy as jnp
from jax import lax
from jax.sharding import PartitionSpec as P

NLB = 8
ATILE = 2


def spread(value, axis, source):
    kept = jnp.where(lax.axis_index(axis) == source, value, 0).astype(value.dtype)
    return lax.psum(kept, axis)


def shards(integrals, panels, screen, owner_map):
    aux_count = lax.axis_size("aux")
    aux_index = lax.axis_index("aux")
    orb_index = lax.axis_index("orb")
    per_owner = panels.shape[0]
    received = []
    for panel_index in range(NLB):
        stored_at = owner_map[panel_index]
        one_panel = lax.dynamic_index_in_dim(panels, stored_at % per_owner, 0, keepdims=False)
        received.append(spread(one_panel, "orb", stored_at // per_owner))
    density = jnp.stack(received, 0)
    group_rows = integrals.shape[1]
    row_count = group_rows // aux_count
    first_row = (orb_index * aux_count + aux_index) * row_count
    keep_rows = lax.dynamic_slice_in_dim(screen, first_row, row_count, 1)
    keep_mask = jnp.repeat(keep_rows, ATILE, axis=0).astype(jnp.bfloat16)
    masked = (
        lax.all_to_all(integrals, "aux", split_axis=1, concat_axis=0, tiled=True)
        * keep_mask[:, :, :, None, None]
    )
    product = jnp.einsum("prjib,jbo->rpio", masked, density, preferred_element_type=jnp.float32)
    halves = product.astype(jnp.bfloat16)
    norm_factor = 1.0 / (halves.shape[1] * halves.shape[3])
    kblocks = (
        jnp.einsum("rpio,rpko->rik", halves, halves, preferred_element_type=jnp.float32)
        * norm_factor
    )
    return (halves, kblocks)


def solution(mesh):
    placed = (P("aux", "orb", None, None, None), P("orb", None, None), P(), P())
    return jax.shard_map(
        shards,
        mesh=mesh,
        in_specs=placed,
        out_specs=(P(("orb", "aux"), None, None, None), P(("orb", "aux"), None, None)),
        check_vma=False,
    )
```

profile of v0, /device:TPU:0, one launch (start us, length us, event | category | flops | bytes accessed | tf_op | source)
XLA Modules:
  0.0 234.2 jit_solution(12756912903240245238)
XLA Ops:
  7.2 10.5 %copy.27 = bf16[2,16,8,128,128]{4,3,2,0,1:T(8,128)(2,1)} copy(bf16[2,16,8,128,128]{4,3,2,1,0:T(8,128)(2,1)} %param.4) | data formatting | bytes 16777216 | tf_op args[0]
  17.7 8.1 %all-to-all-start = ((bf16[2,16,8,128,128]{4,3,2,0,1:T(8,128)(2,1)}), bf16[2,16,8,128,128]{4,3,2,0,1:T(8,128)(2,1)}, u32[]{:S(2)}, u32[]{:S(2)}) async-start(bf16[2,16,8,128,128]{4,3,2,0,1:T(8,128)(2,1)} %copy.27), calls=%async_computation | async-start | bytes 16777216 | tf_op jit(solution)/shard_map/all_to_all | solution.py:32
  25.9 0.2 all-reduce.3.cloned.1.call-start
  26.1 0.7 fusion.12
  31.8 0.3 copy.19
  32.0 2.0 broadcast_select_fusion
  34.0 0.0 all-reduce.3.cloned.1.call-update
  34.0 0.1 constant_dynamic-slice_fusion
  34.1 0.1 copy.36
  34.3 0.1 copy.29
  34.3 75.2 %all-reduce.3.cloned.1.call-done = (bf16[1,128,1920]{1,2,0:T(8,128)(2,1)}, bf16[1,128,1920]{1,2,0:T(8,128)(2,1)}, bf16[1,128,1920]{1,2,0:T(8,128)(2,1)}, bf16[1,...) async-done(((bf16[1,128,1920]{1,2,0:T(8,128)(2,1)}, ...) | async-done | bytes 3932176 | tf_op jit(solution)/shard_map/psum | solution.py:12
  109.5 2.0 constant_dynamic-update-slice_fusion.7
  111.5 1.9 constant_dynamic-update-slice_fusion.6
  113.4 1.9 constant_dynamic-update-slice_fusion.5
  115.3 1.8 constant_dynamic-update-slice_fusion.4
  117.1 0.8 constant_dynamic-update-slice_fusion.3
  117.9 0.8 constant_dynamic-update-slice_fusion.2
  118.8 0.8 constant_dynamic-update-slice_fusion.1
  119.6 0.8 constant_dynamic-update-slice_fusion
  120.4 53.2 %all-to-all-done = bf16[2,16,8,128,128]{4,3,2,0,1:T(8,128)(2,1)} async-done(((bf16[2,16,8,128,128]{4,3,2,0,1:T(8,128)(2,1)}), bf16[2,16,8,128,128]{4,3,2,0,1:T(8,128)(2,1)}, u32[]{:S(2)}, u32[]{:S(2)}) %all-to-all-start) | async-done | bytes 8388640 | tf_op jit(solution)/shard_map/all_to_all | solution.py:32
  173.6 7.4 %bitcast_multiply_fusion = bf16[32,8,128,128]{3,2,1,0:T(8,128)(2,1)} fusion(bf16[2,16,8,128,128]{4,3,2,0,1:T(8,128)(2,1)} %all-to-all-done, bf16[32,8]{1,0:T(8,128)(2,1)S(1)} %bitcast.46), kind=kLoop, calls=%fused_computation.3 | loop fusion | flops 4194304 | bytes 16777728 | tf_op jit(solution)/shard_map/mul | solution.py:32
  180.9 20.0 %bitcast_convert_fusion = bf16[1920,32,128]{2,0,1:T(8,128)(2,1)S(1)} fusion(bf16[32,8,128,128]{3,2,1,0:T(8,128)(2,1)} %bitcast_multiply_fusion, bf16[8,128,1920]{1,2,0:T(8,128)(2,1)} %constant_dynamic-update-slice_fusion), kind=kOutput, calls=%fused_computation | convolution fusion | flops 16113991680 | bytes 28049408 | tf_op jit(solution)/shard_map/prjib,jbo->rpio/dot_general | solution.py:35
  200.9 5.8 %fusion.9 = f32[1,128,128]{2,1,0:T(8,128)} fusion(bf16[1920,32,128]{2,0,1:T(8,128)(2,1)S(1)} %bitcast_convert_fusion), kind=kOutput, calls=%fused_computation.7 | convolution fusion | flops 2013282304 | bytes 15794176 | tf_op jit(solution)/shard_map/rpio,rpko->rik/dot_general | solution.py:39
  206.7 20.7 %copy.32 = bf16[1,32,128,1920]{3,2,1,0:T(8,128)(2,1)} copy(bf16[1,32,128,1920]{2,3,1,0:T(8,128)(2,1)} %bitcast.45) | data formatting | bytes 31457280
  (20 shorter events, 0.1 us)
Async XLA Ops:
  7.2 26.9 %copy-start = (s32[16,128,8]{1,2,0:T(8,128)S(1)}, s32[16,128,8]{1,2,0:T(8,128)}, u32[]{:S(2)}) copy-start(s32[16,128,8]{1,2,0:T(8,128)} %param.6) | copy-start | bytes 196612
  17.7 8.4 %copy-start.8 = (s32[8]{0:T(128)S(1)}, s32[8]{0:T(128)}, u32[]{:S(2)}) copy-start(s32[8]{0:T(128)} %param.7) | copy-start | bytes 100
  17.7 14.0 %copy-start.3 = (bf16[1,128,1920]{2,1,0:T(8,128)(2,1)S(1)}, bf16[1,128,1920]{2,1,0:T(8,128)(2,1)}, u32[]{:S(2)}) copy-start(bf16[1,128,1920]{2,1,0:T(8,128)(2,1)} %param.5) | copy-start | bytes 1474564
  17.7 155.8 %all-to-all-start = ((bf16[2,16,8,128,128]{4,3,2,0,1:T(8,128)(2,1)}), bf16[2,16,8,128,128]{4,3,2,0,1:T(8,128)(2,1)}, u32[]{:S(2)}, u32[]{:S(2)}) async-start(bf16[2,16,8,128,128]{4,3,2,0,1:T(8,128)(2,1)} %copy.27), calls=%async_computation | async-start | bytes 16777216 | tf_op jit(solution)/shard_map/all_to_all | solution.py:32
  25.9 83.6 %all-reduce.3.cloned.1.call-start = ((), (), s32[]{:S(2)}) async-start(), calls=%async_computation.1 | async-start | bytes 7864320 | tf_op jit(solution)/shard_map/psum | solution.py:12
  109.5 7.6 %copy-start.7 = (bf16[1,128,1920]{1,2,0:T(8,128)(2,1)S(1)}, bf16[1,128,1920]{1,2,0:T(8,128)(2,1)}, u32[]{:S(2)}) copy-start(bf16[1,128,1920]{1,2,0:T(8,128)(2,1)} %get-tuple-element.10) | copy-start | bytes 1474564
  109.5 8.4 %copy-start.6 = (bf16[1,128,1920]{1,2,0:T(8,128)(2,1)S(1)}, bf16[1,128,1920]{1,2,0:T(8,128)(2,1)}, u32[]{:S(2)}) copy-start(bf16[1,128,1920]{1,2,0:T(8,128)(2,1)} %get-tuple-element.11) | copy-start | bytes 1474564
  109.5 9.2 %copy-start.5 = (bf16[1,128,1920]{1,2,0:T(8,128)(2,1)S(1)}, bf16[1,128,1920]{1,2,0:T(8,128)(2,1)}, u32[]{:S(2)}) copy-start(bf16[1,128,1920]{1,2,0:T(8,128)(2,1)} %get-tuple-element.12) | copy-start | bytes 1474564
  109.5 10.0 %copy-start.4 = (bf16[1,128,1920]{1,2,0:T(8,128)(2,1)S(1)}, bf16[1,128,1920]{1,2,0:T(8,128)(2,1)}, u32[]{:S(2)}) copy-start(bf16[1,128,1920]{1,2,0:T(8,128)(2,1)} %get-tuple-element.13) | copy-start | bytes 1474564
  200.9 5.8 %copy-start.2 = (bf16[1920,32,128]{2,0,1:T(8,128)(2,1)}, bf16[1920,32,128]{2,0,1:T(8,128)(2,1)S(1)}, u32[]{:S(2)}) copy-start(bf16[1920,32,128]{2,0,1:T(8,128)(2,1)S(1)} %bitcast_convert_fusion) | copy-start | bytes 47185924
  206.7 20.7 %copy-start.1 = (s32[16,128,8]{1,2,0:T(8,128)S(1)}, s32[16,128,8]{1,2,0:T(8,128)}, u32[]{:S(2)}) copy-start(s32[16,128,8]{1,2,0:T(8,128)} %param.6) | copy-start | bytes 196612
Sparse Core Ops, SparseCore 0:
  34.1 75.3 all-reduce.2
where the time goes:
time: 236 us; the launch traced here: 234 us
  waiting for transfers between devices  128 us (54%)
  local copies, waits for them, and re-layouts  43.4 us (18%)
  matrix products  25.8 us (11%)
  between operations  19.1 us (8%)
  other arithmetic  9.35 us (4%)
  starting transfers between devices  8.37 us (4%)
    psum x1, waiting for transfers between devices, spread(): return lax.psum(kept, axis)  75.2 us
    all_to_all x1, waiting for transfers between devices, shards(): lax.all_to_all(integrals, 'aux', split_axis=1, concat_axis=0, tiled=True)  53.2 us
    unnamed x29, local copies, waits for them, and re-layouts  41.7 us
    dot_general x1, matrix products, shards(): jnp.einsum('prjib,jbo->rpio', masked, density, preferred_element_type=jnp...  20 us
    all_to_all x1, starting transfers between devices, shards(): lax.all_to_all(integrals, 'aux', split_axis=1, concat_axis=0, tiled=True)  8.14 us
    mul x1, other arithmetic, shards(): lax.all_to_all(integrals, 'aux', split_axis=1, concat_axis=0, tiled=True)  7.39 us
    dot_general x1, matrix products, shards(): jnp.einsum('rpio,rpko->rik', halves, halves, preferred_element_type=jnp.f...  5.79 us
  transfers between devices with their start and end apart: 2, of which 2 were waited for; matrix products, arithmetic and copies ran while one was open for 6% of the time, Pallas kernels for 0%

commit v1 on v0

v1 whole, which is shorter than its diff:
```python
import functools

import jax
import jax.numpy as jnp
from jax import lax
from jax.experimental import pallas as pl
from jax.experimental.pallas import tpu as pltpu
from jax.sharding import PartitionSpec as P

MESH = pl.DeviceIdType.MESH
BS = 128
NLB = 8
NOCC = 1920
NAUX = 32
NAT = 16
NRB = 128
DEPTH = NLB * BS
SIDE = 4
SCALE = 1.0 / (NAUX * NOCC)
ORDER = (2, 3, 1)
COLUMNS = ((0, 512), (512, 512), (1024, 512), (1536, 384))
EARLY = [(0, 0)] + [(d, 0) for d in ORDER] + [(0, e) for e in ORDER] + [(d, 2) for d in ORDER] + [(2, 3), (2, 1), (3, 3), (3, 1)]
LATE = [(1, 3), (1, 1)]


def place():
    a, o = lax.axis_index("aux"), lax.axis_index("orb")
    return a // SIDE, a % SIDE, o // 2, o % 2


def tile_of(x, z, dx, dz):
    return (x + SIDE - dx) % SIDE * SIDE + (z + SIDE - dz) % SIDE


def transform(x, z, d, e, fin_ref, mask_ref, dens_ref, lhs, put):
    for p, (dx, dz) in ((0, (d, e)), (1, (e, d))):
        keep = mask_ref[pl.ds(tile_of(x, z, dx, dz), 1), :]
        for j in range(NLB):
            block = fin_ref[p, dx, dz, j].astype(jnp.float32) * keep[:, j * BS : (j + 1) * BS]
            lhs[p * BS : (p + 1) * BS, j * BS : (j + 1) * BS] = block.astype(jnp.bfloat16)
    for at, width in COLUMNS:
        product = jnp.dot(lhs[...], dens_ref[:, at : at + width], preferred_element_type=jnp.float32)
        put(at, width, product.astype(jnp.bfloat16))


def gram(half):
    return lax.dot_general(half, half, (((1,), (1,)), ((), ())), preferred_element_type=jnp.float32)


def gather_kernel(
    ints, panel, screen, owner, hv, fin, dens, mask, kacc,
    xa, zb, prcv, scr, own, lhs, s_one, r_one, s_two, r_fin, s_pan, r_pan, l_sem,
):
    x, z, y, c = place()
    o = y * 2 + c

    def at_xz(dx, dz):
        return ((x + dx) % SIDE * SIDE + (z + dz) % SIDE, o)

    def at_orb(dy, dc):
        return (x * SIDE + z, (y + dy) % SIDE * 2 + (c + dc) % 2)

    def send(src, dst, ss, rs, to):
        return pltpu.make_async_remote_copy(
            src_ref=src, dst_ref=dst, send_sem=ss, recv_sem=rs, device_id=to, device_id_type=MESH
        )

    barrier = pltpu.get_barrier_semaphore()
    for d in (1, 2, 3):
        for to in (at_xz(d, 0), at_xz(0, d), at_orb(d, 0)):
            pl.semaphore_signal(barrier, inc=1, device_id=to, device_id_type=MESH)
    pl.semaphore_signal(barrier, inc=1, device_id=at_orb(0, 1), device_id_type=MESH)
    pl.semaphore_wait(barrier, 10)

    relay_a, relay_b = {}, {}
    for d in ORDER:
        for e in ORDER:
            relay_a[d, e] = send(ints.at[0, (x + d) % SIDE, (z + e) % SIDE], xa.at[d - 1, e - 1], s_one.at[0, d, e], r_one.at[0, d, e], at_xz(d, 0))
            relay_b[d, e] = send(ints.at[1, (x + e) % SIDE, (z + d) % SIDE], zb.at[d - 1, e - 1], s_one.at[1, d, e], r_one.at[1, d, e], at_xz(0, d))
            relay_a[d, e].start()
            relay_b[d, e].start()
    panels = {d: send(panel.at[0], prcv.at[o], s_pan.at[0, d], r_pan.at[0, d], at_orb(d, 0)) for d in ORDER}
    for d in ORDER:
        panels[d].start()
    direct = []
    for d in ORDER:
        direct.append(send(ints.at[0, (x + d) % SIDE, z], fin.at[0, d, 0], s_one.at[0, d, 0], r_fin.at[0, d, 0], at_xz(d, 0)))
        direct.append(send(ints.at[1, x, (z + d) % SIDE], fin.at[1, 0, d], s_one.at[1, d, 0], r_fin.at[1, d, 0], at_xz(0, d)))
    for e in ORDER:
        direct.append(send(ints.at[0, x, (z + e) % SIDE], fin.at[0, 0, e], s_two.at[0, 0, e], r_fin.at[0, 0, e], at_xz(0, e)))
        direct.append(send(ints.at[1, (x + e) % SIDE, z], fin.at[1, e, 0], s_two.at[1, 0, e], r_fin.at[1, 0, e], at_xz(e, 0)))
    for copy in direct:
        copy.start()
    mine = [
        pltpu.make_async_copy(ints.at[0, x, z], fin.at[0, 0, 0], l_sem.at[0]),
        pltpu.make_async_copy(ints.at[1, x, z], fin.at[1, 0, 0], l_sem.at[1]),
        pltpu.make_async_copy(panel.at[0], prcv.at[o], l_sem.at[2]),
    ]
    row = o * SIDE * SIDE + x * SIDE + z
    masks = pltpu.make_async_copy(screen, scr, l_sem.at[3])
    masks.start()
    owners = pltpu.make_async_copy(owner, own, l_sem.at[4])
    owners.start()
    for copy in mine:
        copy.start()
    shared = {0: send(panel.at[0], prcv.at[o], s_pan.at[1, 0], r_pan.at[1, 0], at_orb(0, 1))}
    shared[0].start()

    masks.wait()
    pick = lax.broadcasted_iota(jnp.int32, (NAT, NLB, NRB), 2) == row
    kept = jnp.sum(jnp.where(pick, scr[...], 0).astype(jnp.float32), axis=2)
    wide = lax.broadcasted_iota(jnp.int32, (NLB, DEPTH), 1) // BS == lax.broadcasted_iota(jnp.int32, (NLB, DEPTH), 0)
    mask[...] = jnp.dot(kept, wide.astype(jnp.float32), preferred_element_type=jnp.float32)
    kacc[...] = jnp.zeros_like(kacc)

    for d in ORDER:
        panels[d].wait_recv()
        slot = (y + SIDE - d) % SIDE * 2 + c
        shared[d] = send(prcv.at[slot], prcv.at[slot], s_pan.at[1, d], r_pan.at[1, d], at_orb(0, 1))
        shared[d].start()

    second = {}
    for d in ORDER:
        for e in ORDER:
            second[0, d, e] = send(xa.at[d - 1, e - 1], fin.at[0, d, e], s_two.at[0, d, e], r_fin.at[0, d, e], at_xz(0, e))
            second[1, d, e] = send(zb.at[d - 1, e - 1], fin.at[1, e, d], s_two.at[1, d, e], r_fin.at[1, d, e], at_xz(e, 0))
    for d in ORDER:
        for e in ORDER:
            relay_a[d, e].wait_recv()
            second[0, d, e].start()
            relay_b[d, e].wait_recv()
            second[1, d, e].start()

    for d in range(SIDE):
        shared[d].wait_recv()
    mine[2].wait()
    owners.wait()
    for j in range(NLB):
        dens[j * BS : (j + 1) * BS, :] = prcv[own[j]]

    def pair(d, e):
        for p, (dx, dz) in ((0, (d, e)), (1, (e, d))):
            send(fin.at[p, dx, dz], fin.at[p, dx, dz], s_one.at[0, 0, 0], r_fin.at[p, d, e], at_xz(1, 0)).wait_recv()

    def work(d, e):
        spots = [tile_of(x, z, d, e) * 2, tile_of(x, z, e, d) * 2 + 1]

        def put(at, width, value):
            for p in range(2):
                hv[pl.ds(spots[p], 1), :, at : at + width] = value[p * BS : (p + 1) * BS].reshape(1, BS, width)

        transform(x, z, d, e, fin, mask, dens, lhs, put)
        for p in range(2):
            kacc[...] += gram(hv[pl.ds(spots[p], 1)].reshape(BS, NOCC))

    mine[0].wait()
    mine[1].wait()
    work(0, 0)

    def step(g, _):
        d, e = pairs(g)
        pair(d, e)
        work(d, e)
        return 0

    lax.fori_loop(0, len(EARLY) - 1, step, 0)
    for d, e in LATE:
        pair(d, e)
    for copy in list(relay_a.values()) + list(relay_b.values()) + direct + list(second.values()) + list(panels.values()) + list(shared.values()):
        copy.wait_send()


def pairs(g):
    first, second, third = g // 3 == 0, g // 3 == 1, g // 3 == 2
    turn = (g + 1) % 3 + 1
    late = g - 9
    d = jnp.where(first | third, turn, jnp.where(second, 0, (late // 2 + 1) % 3 + 1))
    e = jnp.where(first, 0, jnp.where(second, turn, jnp.where(third, 2, 3 - late % 2 * 2)))
    return d, e


def finish_kernel(hv, fin, dens, mask, kacc, halves, kblocks, lhs, late, sems):
    x, z, y, c = place()

    def out(source, spot):
        return pltpu.make_async_copy(source, halves.at[0, spot], sems.at[spot])

    copies = []
    for d, e in EARLY:
        for p, (dx, dz) in ((0, (d, e)), (1, (e, d))):
            spot = tile_of(x, z, dx, dz) * 2 + p
            copies.append(out(hv.at[spot], spot))
            copies[-1].start()
    total = kacc[...]
    for k, (d, e) in enumerate(LATE):

        def put(at, width, value):
            for p in range(2):
                late[2 * k + p, :, at : at + width] = value[p * BS : (p + 1) * BS]

        transform(x, z, d, e, fin, mask, dens, lhs, put)
        for p, (dx, dz) in ((0, (d, e)), (1, (e, d))):
            spot = tile_of(x, z, dx, dz) * 2 + p
            copies.append(out(late.at[2 * k + p], spot))
            copies[-1].start()
            total += gram(late[2 * k + p])
    kblocks[0] = total * SCALE
    for copy in copies:
        copy.wait()


def shards(integrals, panels, screen, owner_map):
    piece = (NLB, BS, BS)
    vmem = pl.BlockSpec(memory_space=pltpu.VMEM)
    hbm = pl.BlockSpec(memory_space=pl.ANY)
    dma = pltpu.SemaphoreType.DMA
    bf16, f32 = jnp.bfloat16, jnp.float32
    ints = integrals.reshape((2, SIDE, SIDE) + piece)
    between = pl.pallas_call(
        gather_kernel,
        name="gather",
        out_shape=[
            pltpu.VMEM((NAUX, BS, NOCC), bf16),
            pltpu.VMEM((2, SIDE, SIDE) + piece, bf16),
            pltpu.VMEM((DEPTH, NOCC), bf16),
            pltpu.VMEM((NAT, DEPTH), f32),
            pltpu.VMEM((BS, BS), f32),
        ],
        in_specs=[hbm] * 4,
        out_specs=[vmem] * 5,
        scratch_shapes=[
            pltpu.VMEM((3, 3) + piece, bf16),
            pltpu.VMEM((3, 3) + piece, bf16),
            pltpu.VMEM((NLB, BS, NOCC), bf16),
            pltpu.VMEM((NAT, NLB, NRB), jnp.int32),
            pltpu.SMEM((NLB,), jnp.int32),
            pltpu.VMEM((2 * BS, DEPTH), bf16),
            dma((2, 4, 4)),
            dma((2, 4, 4)),
            dma((2, 4, 4)),
            dma((2, 4, 4)),
            dma((2, 4)),
            dma((2, 4)),
            dma((5,)),
        ],
        compiler_params=pltpu.CompilerParams(collective_id=0, has_side_effects=True, vmem_limit_bytes=24 << 20),
        cost_estimate=pl.CostEstimate(flops=16 << 30, bytes_accessed=24 << 20, transcendentals=0),
    )(*(pltpu.with_memory_space_constraint(v, pltpu.HBM) for v in (ints, panels, screen.transpose(0, 2, 1), owner_map)))
    return pl.pallas_call(
        finish_kernel,
        name="finish",
        out_shape=[
            jax.ShapeDtypeStruct((1, NAUX, BS, NOCC), bf16),
            jax.ShapeDtypeStruct((1, BS, BS), f32),
        ],
        in_specs=[vmem] * 5,
        out_specs=[hbm, vmem],
        scratch_shapes=[
            pltpu.VMEM((2 * BS, DEPTH), bf16),
            pltpu.VMEM((2 * len(LATE), BS, NOCC), bf16),
            dma((NAUX,)),
        ],
        compiler_params=pltpu.CompilerParams(vmem_limit_bytes=24 << 20),
        cost_estimate=pl.CostEstimate(flops=2 << 30, bytes_accessed=16 << 20, transcendentals=0),
    )(*(pltpu.with_memory_space_constraint(v, pltpu.VMEM) for v in between))


def solution(mesh):
    placed = (P("aux", "orb", None, None, None), P("orb", None, None), P(), P())
    return jax.shard_map(
        shards,
        mesh=mesh,
        in_specs=placed,
        out_specs=(P(("orb", "aux"), None, None, None), P(("orb", "aux"), None, None)),
        check_vma=False,
    )
```

time: 236 us -> 113 us (0.48)
  waiting for transfers between devices: 128 us -> 0 us
  Pallas kernels: 0 us -> 112 us
  local copies, waits for them, and re-layouts: 43.4 us -> 0 us
  matrix products: 25.8 us -> 0 us
  between operations: 19.1 us -> 0.64 us
  other arithmetic: 9.35 us -> 0 us
  starting transfers between devices: 8.37 us -> 0 us
    pallas_call x0 -> x2, Pallas kernels: none -> 112 us  [the longest x1 104 us: shards(): pl.pallas_call(gather_kernel, name='gather', out_shape=[pltpu.VMEM((NAUX,...]
    psum x1 -> x0, waiting for transfers between devices: 75.2 us -> none  [spread(): return lax.psum(kept, axis)]
    all_to_all x1 -> x0, waiting for transfers between devices: 53.2 us -> none  [shards(): lax.all_to_all(integrals, 'aux', split_axis=1, concat_axis=0, tiled=True)]
    unnamed x29 -> x0, local copies, waits for them, and re-layouts: 41.7 us -> none
    dot_general x2 -> x0, matrix products: 25.8 us -> none  [the longest x1 20 us: shards(): jnp.einsum('prjib,jbo->rpio', masked, density, preferred_element_type=jnp...]
    all_to_all x1 -> x0, starting transfers between devices: 8.14 us -> none  [shards(): lax.all_to_all(integrals, 'aux', split_axis=1, concat_axis=0, tiled=True)]
    mul x1 -> x0, other arithmetic: 7.39 us -> none  [shards(): lax.all_to_all(integrals, 'aux', split_axis=1, concat_axis=0, tiled=True)]
  transfers between devices with their start and end apart: 2 -> 0, of which waited for: 2 -> 0; matrix products, arithmetic and copies ran while one was open for 6% -> 0% of each run, Pallas kernels for 0% -> 0%
where the time goes in v1:
time: 113 us; the launch traced here: 112 us
  Pallas kernels  112 us (99%)
    pallas_call x1, Pallas kernels, shards(): pl.pallas_call(gather_kernel, name='gather', out_shape=[pltpu.VMEM((NAUX,...  104 us
    pallas_call x1, Pallas kernels, shards(): pl.pallas_call(finish_kernel, name='finish', out_shape=[jax.ShapeDtypeStr...  8.06 us

profile of v1, /device:TPU:0, one launch (start us, length us, event | category | flops | bytes accessed | tf_op | source)
XLA Modules:
  0.0 112.4 jit_solution(6041531715693709381)
XLA Ops:
  0.6 103.7 %gather.1 = (bf16[32,128,1920]{2,1,0:T(8,128)(2,1)S(1)}, bf16[2,4,4,8,128,128]{5,4,3,2,1,0:T(8,128)(2,1)S(1)}, bf16[1024,1920]{1,0:T(8,128)(2,1)S(1)}, f32[16,1024]{1,0:T(8,128)S(1)}, f32[128,128]{1,0:T(8,128)S(1)}) custom-call(bf16[2,4,4,8,128,128]{5,4,3,2,1,0:T(8,128)(2,1)} %bitcast.2, bf16[1,128,1920]{2,1,0:T(8,128)(2,1)} %panel.1, ...), custom_call_target="tpu_custom_call" | custom-call | flops 17179869184 | bytes 25165824 | tf_op jit(solution)/shard_map/gather/pallas_call | solution.py:219
  104.3 8.1 %finish.1 = (bf16[1,32,128,1920]{3,2,1,0:T(8,128)(2,1)}, f32[1,128,128]{2,1,0:T(8,128)}) custom-call(bf16[32,128,1920]{2,1,0:T(8,128)(2,1)S(1)} %get-tuple-element.7.hv, bf16[2,4,4,8,128,128]{5,4,3,2,1,0:T(8,128)(2,1)S(1)} %get-tuple-element.8.fin, bf16[1024,1920]{1,0:T(8,128)(2,1)S(1)} %get-tuple-element.9.dens, f32[16,1024]{1,0:T(8,128)S(1)} %get-tuple-element.10.mask, ...), custom_call_target="tpu_custom_call" | custom-call | flops 2147483648 | bytes 16777216 | tf_op jit(solution)/shard_map/finish/pallas_call | solution.py:249

commit v2 on v1

--- a/solution.py
+++ b/solution.py
@@ -18,6 +18,7 @@
 SIDE = 4
 SCALE = 1.0 / (NAUX * NOCC)
 ORDER = (2, 3, 1)
+STEP = 640
 COLUMNS = ((0, 512), (512, 512), (1024, 512), (1536, 384))
 EARLY = [(0, 0)] + [(d, 0) for d in ORDER] + [(0, e) for e in ORDER] + [(d, 2) for d in ORDER] + [(2, 3), (2, 1), (3, 3), (3, 1)]
 LATE = [(1, 3), (1, 1)]
@@ -32,15 +33,12 @@
     return (x + SIDE - dx) % SIDE * SIDE + (z + SIDE - dz) % SIDE
 
 
-def transform(x, z, d, e, fin_ref, mask_ref, dens_ref, lhs, put):
-    for p, (dx, dz) in ((0, (d, e)), (1, (e, d))):
-        keep = mask_ref[pl.ds(tile_of(x, z, dx, dz), 1), :]
-        for j in range(NLB):
-            block = fin_ref[p, dx, dz, j].astype(jnp.float32) * keep[:, j * BS : (j + 1) * BS]
-            lhs[p * BS : (p + 1) * BS, j * BS : (j + 1) * BS] = block.astype(jnp.bfloat16)
-    for at, width in COLUMNS:
-        product = jnp.dot(lhs[...], dens_ref[:, at : at + width], preferred_element_type=jnp.float32)
-        put(at, width, product.astype(jnp.bfloat16))
+def fill(p, dx, dz, x, z, fin_ref, mask_ref, lhs, k):
+    keep = mask_ref[pl.ds(tile_of(x, z, dx, dz), 1), :]
+    rows = pl.ds(pl.multiple_of(k * BS, BS), BS)
+    for j in range(NLB):
+        block = fin_ref[p, dx, dz, j].astype(jnp.float32) * keep[:, j * BS : (j + 1) * BS]
+        lhs[rows, j * BS : (j + 1) * BS] = block.astype(jnp.bfloat16)
 
 
 def gram(half):
@@ -124,12 +122,11 @@
         for e in ORDER:
             second[0, d, e] = send(xa.at[d - 1, e - 1], fin.at[0, d, e], s_two.at[0, d, e], r_fin.at[0, d, e], at_xz(0, e))
             second[1, d, e] = send(zb.at[d - 1, e - 1], fin.at[1, e, d], s_two.at[1, d, e], r_fin.at[1, d, e], at_xz(e, 0))
-    for d in ORDER:
-        for e in ORDER:
-            relay_a[d, e].wait_recv()
-            second[0, d, e].start()
-            relay_b[d, e].wait_recv()
-            second[1, d, e].start()
+    for d, e in EARLY[7:] + LATE:
+        relay_a[d, e].wait_recv()
+        second[0, d, e].start()
+        relay_b[d, e].wait_recv()
+        second[1, d, e].start()
 
     for d in range(SIDE):
         shared[d].wait_recv()
@@ -144,12 +141,13 @@
 
     def work(d, e):
         spots = [tile_of(x, z, d, e) * 2, tile_of(x, z, e, d) * 2 + 1]
-
-        def put(at, width, value):
+        fill(0, d, e, x, z, fin, mask, lhs, 0)
+        fill(1, e, d, x, z, fin, mask, lhs, 1)
+        for at, width in COLUMNS:
+            product = jnp.dot(lhs[...], dens[:, at : at + width], preferred_element_type=jnp.float32)
+            product = product.astype(jnp.bfloat16)
             for p in range(2):
-                hv[pl.ds(spots[p], 1), :, at : at + width] = value[p * BS : (p + 1) * BS].reshape(1, BS, width)
-
-        transform(x, z, d, e, fin, mask, dens, lhs, put)
+                hv[pl.ds(spots[p], 1), :, at : at + width] = product[p * BS : (p + 1) * BS].reshape(1, BS, width)
         for p in range(2):
             kacc[...] += gram(hv[pl.ds(spots[p], 1)].reshape(BS, NOCC))
 
@@ -181,29 +179,47 @@
 
 def finish_kernel(hv, fin, dens, mask, kacc, halves, kblocks, lhs, late, sems):
     x, z, y, c = place()
-
-    def out(source, spot):
-        return pltpu.make_async_copy(source, halves.at[0, spot], sems.at[spot])
-
     copies = []
-    for d, e in EARLY:
-        for p, (dx, dz) in ((0, (d, e)), (1, (e, d))):
-            spot = tile_of(x, z, dx, dz) * 2 + p
-            copies.append(out(hv.at[spot], spot))
-            copies[-1].start()
-    total = kacc[...]
-    for k, (d, e) in enumerate(LATE):
-
-        def put(at, width, value):
-            for p in range(2):
-                late[2 * k + p, :, at : at + width] = value[p * BS : (p + 1) * BS]
-
-        transform(x, z, d, e, fin, mask, dens, lhs, put)
-        for p, (dx, dz) in ((0, (d, e)), (1, (e, d))):
-            spot = tile_of(x, z, dx, dz) * 2 + p
-            copies.append(out(late.at[2 * k + p], spot))
-            copies[-1].start()
-            total += gram(late[2 * k + p])
+
+    def out(source, spot, count):
+        copies.append(pltpu.make_async_copy(source, halves.at[0, pl.ds(spot, count)], sems.at[len(copies)]))
+        copies[-1].start()
+
+    left = [unit for d, e in LATE for unit in ((0, d, e), (1, e, d))]
+    whole = [dx for dx in range(SIDE) if all(dx != unit[1] for unit in left)]
+    for dx in whole:
+        spot = (x + SIDE - dx) % SIDE * SIDE * 2
+        out(hv.at[pl.ds(spot, 2 * SIDE)], spot, 2 * SIDE)
+    rest = []
+    for dx in range(SIDE):
+        for dz in range(SIDE):
+            ready = [p for p in range(2) if (p, dx, dz) not in left]
+            if ready and dx not in whole:
+                rest.append((tile_of(x, z, dx, dz) * 2 + ready[0], len(ready)))
+    for spot, count in rest:
+        out(hv.at[pl.ds(spot, count)], spot, count)
+
+    def unit(k):
+        d, e, p = 1, 3 - k // 2 * 2, k % 2
+        return p, (1 - p) * d + p * e, (1 - p) * e + p * d
+
+    def stage(k, _):
+        p, dx, dz = unit(k)
+        fill(p, dx, dz, x, z, fin, mask, lhs, k)
+        return 0
+
+    def column(i, _):
+        at = pl.multiple_of(i * STEP, STEP)
+        product = jnp.dot(lhs[...], dens[:, pl.ds(at, STEP)], preferred_element_type=jnp.float32)
+        late[:, :, pl.ds(at, STEP)] = product.astype(jnp.bfloat16).reshape(len(left), BS, STEP)
+        return 0
+
+    lax.fori_loop(0, len(left), stage, 0)
+    lax.fori_loop(0, NOCC // STEP, column, 0)
+    for k in range(len(left)):
+        p, dx, dz = unit(k)
+        out(late.at[pl.ds(k, 1)], tile_of(x, z, dx, dz) * 2 + p, 1)
+    total = lax.fori_loop(0, len(left), lambda k, total: total + gram(late[k]), kacc[...])
     kblocks[0] = total * SCALE
     for copy in copies:
         copy.wait()
@@ -256,7 +272,7 @@
         in_specs=[vmem] * 5,
         out_specs=[hbm, vmem],
         scratch_shapes=[
-            pltpu.VMEM((2 * BS, DEPTH), bf16),
+            pltpu.VMEM((2 * len(LATE) * BS, DEPTH), bf16),
             pltpu.VMEM((2 * len(LATE), BS, NOCC), bf16),
             dma((NAUX,)),
         ],

time: 113 us -> 107 us (0.947)
  Pallas kernels: 112 us -> 106 us
    pallas_call x1, Pallas kernels: 104 us -> 99.2 us  [shards(): pl.pallas_call(gather_kernel, name='gather', out_shape=[pltpu.VMEM((NAUX,...]
    pallas_call x1, Pallas kernels: 8.06 us -> 6.52 us  [shards(): pl.pallas_call(finish_kernel, name='finish', out_shape=[jax.ShapeDtypeStr...]
where the time goes in v2:
time: 107 us; the launch traced here: 106 us
  Pallas kernels  106 us (99%)
    pallas_call x1, Pallas kernels, shards(): pl.pallas_call(gather_kernel, name='gather', out_shape=[pltpu.VMEM((NAUX,...  99.2 us
    pallas_call x1, Pallas kernels, shards(): pl.pallas_call(finish_kernel, name='finish', out_shape=[jax.ShapeDtypeStr...  6.52 us

profile of v2, /device:TPU:0, one launch (start us, length us, event | category | flops | bytes accessed | tf_op | source)
XLA Modules:
  0.0 106.4 jit_solution(10441039539315257890)
XLA Ops:
  0.6 99.2 %gather.1 = (bf16[32,128,1920]{2,1,0:T(8,128)(2,1)S(1)}, bf16[2,4,4,8,128,128]{5,4,3,2,1,0:T(8,128)(2,1)S(1)}, bf16[1024,1920]{1,0:T(8,128)(2,1)S(1)}, f32[16,1024]{1,0:T(8,128)S(1)}, f32[128,128]{1,0:T(8,128)S(1)}) custom-call(bf16[2,4,4,8,128,128]{5,4,3,2,1,0:T(8,128)(2,1)} %bitcast.2, bf16[1,128,1920]{2,1,0:T(8,128)(2,1)} %panel.1, ...), custom_call_target="tpu_custom_call" | custom-call | flops 17179869184 | bytes 25165824 | tf_op jit(solution)/shard_map/gather/pallas_call | solution.py:235
  99.9 6.5 %finish.1 = (bf16[1,32,128,1920]{3,2,1,0:T(8,128)(2,1)}, f32[1,128,128]{2,1,0:T(8,128)}) custom-call(bf16[32,128,1920]{2,1,0:T(8,128)(2,1)S(1)} %get-tuple-element.7.hv, bf16[2,4,4,8,128,128]{5,4,3,2,1,0:T(8,128)(2,1)S(1)} %get-tuple-element.8.fin, bf16[1024,1920]{1,0:T(8,128)(2,1)S(1)} %get-tuple-element.9.dens, f32[16,1024]{1,0:T(8,128)S(1)} %get-tuple-element.10.mask, ...), custom_call_target="tpu_custom_call" | custom-call | flops 2147483648 | bytes 16777216 | tf_op jit(solution)/shard_map/finish/pallas_call | solution.py:265

commit v3 on v2

--- a/solution.py
+++ b/solution.py
@@ -20,8 +20,8 @@
 ORDER = (2, 3, 1)
 STEP = 640
 COLUMNS = ((0, 512), (512, 512), (1024, 512), (1536, 384))
-EARLY = [(0, 0)] + [(d, 0) for d in ORDER] + [(0, e) for e in ORDER] + [(d, 2) for d in ORDER] + [(2, 3), (2, 1), (3, 3), (3, 1)]
-LATE = [(1, 3), (1, 1)]
+PAIRS = [(d, 0) for d in (0,) + ORDER] + [(d, e) for d in (0,) + ORDER for e in ORDER]
+EARLY, LATE = PAIRS[:14], PAIRS[14:]
 
 
 def place():
@@ -47,7 +47,7 @@
 
 def gather_kernel(
     ints, panel, screen, owner, hv, fin, dens, mask, kacc,
-    xa, zb, prcv, scr, own, lhs, s_one, r_one, s_two, r_fin, s_pan, r_pan, l_sem,
+    xa, zb, prcv, scr, own, lhs, s_one, r_one, s_two, r_fin, s_pan, r_pan, l_sem, d_sem,
 ):
     x, z, y, c = place()
     o = y * 2 + c
@@ -72,18 +72,14 @@
 
     relay_a, relay_b = {}, {}
     for d in ORDER:
-        for e in ORDER:
-            relay_a[d, e] = send(ints.at[0, (x + d) % SIDE, (z + e) % SIDE], xa.at[d - 1, e - 1], s_one.at[0, d, e], r_one.at[0, d, e], at_xz(d, 0))
-            relay_b[d, e] = send(ints.at[1, (x + e) % SIDE, (z + d) % SIDE], zb.at[d - 1, e - 1], s_one.at[1, d, e], r_one.at[1, d, e], at_xz(0, d))
-            relay_a[d, e].start()
-            relay_b[d, e].start()
+        relay_a[d] = send(ints.at[0, (x + d) % SIDE], xa.at[d - 1], s_one.at[0, d], r_one.at[0, d], at_xz(d, 0))
+        relay_b[d] = send(ints.at[1, :, (z + d) % SIDE], zb.at[d - 1], s_one.at[1, d], r_one.at[1, d], at_xz(0, d))
+        relay_a[d].start()
+        relay_b[d].start()
     panels = {d: send(panel.at[0], prcv.at[o], s_pan.at[0, d], r_pan.at[0, d], at_orb(d, 0)) for d in ORDER}
     for d in ORDER:
         panels[d].start()
     direct = []
-    for d in ORDER:
-        direct.append(send(ints.at[0, (x + d) % SIDE, z], fin.at[0, d, 0], s_one.at[0, d, 0], r_fin.at[0, d, 0], at_xz(d, 0)))
-        direct.append(send(ints.at[1, x, (z + d) % SIDE], fin.at[1, 0, d], s_one.at[1, d, 0], r_fin.at[1, d, 0], at_xz(0, d)))
     for e in ORDER:
         direct.append(send(ints.at[0, x, (z + e) % SIDE], fin.at[0, 0, e], s_two.at[0, 0, e], r_fin.at[0, 0, e], at_xz(0, e)))
         direct.append(send(ints.at[1, (x + e) % SIDE, z], fin.at[1, e, 0], s_two.at[1, 0, e], r_fin.at[1, 0, e], at_xz(e, 0)))
@@ -119,25 +115,29 @@
 
     second = {}
     for d in ORDER:
+        relay_a[d].wait_recv()
+        relay_b[d].wait_recv()
         for e in ORDER:
-            second[0, d, e] = send(xa.at[d - 1, e - 1], fin.at[0, d, e], s_two.at[0, d, e], r_fin.at[0, d, e], at_xz(0, e))
-            second[1, d, e] = send(zb.at[d - 1, e - 1], fin.at[1, e, d], s_two.at[1, d, e], r_fin.at[1, d, e], at_xz(e, 0))
-    for d, e in EARLY[7:] + LATE:
-        relay_a[d, e].wait_recv()
-        second[0, d, e].start()
-        relay_b[d, e].wait_recv()
-        second[1, d, e].start()
+            second[0, d, e] = send(xa.at[d - 1, (z + e) % SIDE], fin.at[0, d, e], s_two.at[0, d, e], r_fin.at[0, d, e], at_xz(0, e))
+            second[1, d, e] = send(zb.at[d - 1, (x + e) % SIDE], fin.at[1, e, d], s_two.at[1, d, e], r_fin.at[1, d, e], at_xz(e, 0))
+            second[0, d, e].start()
+            second[1, d, e].start()
+        mine.append(pltpu.make_async_copy(xa.at[d - 1, z], fin.at[0, d, 0], d_sem.at[0, d]))
+        mine.append(pltpu.make_async_copy(zb.at[d - 1, x], fin.at[1, 0, d], d_sem.at[1, d]))
+        mine[-2].start()
+        mine[-1].start()
 
     for d in range(SIDE):
         shared[d].wait_recv()
-    mine[2].wait()
+    for copy in mine:
+        copy.wait()
     owners.wait()
     for j in range(NLB):
         dens[j * BS : (j + 1) * BS, :] = prcv[own[j]]
 
     def pair(d, e):
         for p, (dx, dz) in ((0, (d, e)), (1, (e, d))):
-            send(fin.at[p, dx, dz], fin.at[p, dx, dz], s_one.at[0, 0, 0], r_fin.at[p, d, e], at_xz(1, 0)).wait_recv()
+            send(fin.at[p, dx, dz], fin.at[p, dx, dz], s_one.at[0, 0], r_fin.at[p, d, e], at_xz(1, 0)).wait_recv()
 
     def work(d, e):
         spots = [tile_of(x, z, d, e) * 2, tile_of(x, z, e, d) * 2 + 1]
@@ -151,33 +151,33 @@
         for p in range(2):
             kacc[...] += gram(hv[pl.ds(spots[p], 1)].reshape(BS, NOCC))
 
-    mine[0].wait()
-    mine[1].wait()
-    work(0, 0)
-
     def step(g, _):
-        d, e = pairs(g)
-        pair(d, e)
+        d, e = pair_at(g)
+
+        @pl.when(g >= SIDE)
+        def _():
+            pair(d, e)
+
         work(d, e)
         return 0
 
-    lax.fori_loop(0, len(EARLY) - 1, step, 0)
+    lax.fori_loop(0, len(EARLY), step, 0)
     for d, e in LATE:
         pair(d, e)
     for copy in list(relay_a.values()) + list(relay_b.values()) + direct + list(second.values()) + list(panels.values()) + list(shared.values()):
         copy.wait_send()
 
 
-def pairs(g):
-    first, second, third = g // 3 == 0, g // 3 == 1, g // 3 == 2
-    turn = (g + 1) % 3 + 1
-    late = g - 9
-    d = jnp.where(first | third, turn, jnp.where(second, 0, (late // 2 + 1) % 3 + 1))
-    e = jnp.where(first, 0, jnp.where(second, turn, jnp.where(third, 2, 3 - late % 2 * 2)))
-    return d, e
-
-
-def finish_kernel(hv, fin, dens, mask, kacc, halves, kblocks, lhs, late, sems):
+def pair_at(g):
+    def turn(i):
+        return (2 * i - i // 2) % SIDE
+
+    h = lax.max(g - SIDE, 0)
+    first = g < SIDE
+    return jnp.where(first, turn(g), turn(h // 3)), jnp.where(first, 0, turn(h % 3 + 1))
+
+
+def finish_kernel(hv, fin, dens, mask, kacc, halves, kblocks, lhs, late, kout, sems, k_sem):
     x, z, y, c = place()
     copies = []
 
@@ -220,7 +220,9 @@
         p, dx, dz = unit(k)
         out(late.at[pl.ds(k, 1)], tile_of(x, z, dx, dz) * 2 + p, 1)
     total = lax.fori_loop(0, len(left), lambda k, total: total + gram(late[k]), kacc[...])
-    kblocks[0] = total * SCALE
+    kout[0] = total * SCALE
+    copies.append(pltpu.make_async_copy(kout, kblocks, k_sem))
+    copies[-1].start()
     for copy in copies:
         copy.wait()
 
@@ -245,19 +247,20 @@
         in_specs=[hbm] * 4,
         out_specs=[vmem] * 5,
         scratch_shapes=[
-            pltpu.VMEM((3, 3) + piece, bf16),
-            pltpu.VMEM((3, 3) + piece, bf16),
+            pltpu.VMEM((3, SIDE) + piece, bf16),
+            pltpu.VMEM((3, SIDE) + piece, bf16),
             pltpu.VMEM((NLB, BS, NOCC), bf16),
             pltpu.VMEM((NAT, NLB, NRB), jnp.int32),
             pltpu.SMEM((NLB,), jnp.int32),
             pltpu.VMEM((2 * BS, DEPTH), bf16),
+            dma((2, 4)),
+            dma((2, 4)),
             dma((2, 4, 4)),
             dma((2, 4, 4)),
-            dma((2, 4, 4)),
-            dma((2, 4, 4)),
             dma((2, 4)),
             dma((2, 4)),
             dma((5,)),
+            dma((2, 4)),
         ],
         compiler_params=pltpu.CompilerParams(collective_id=0, has_side_effects=True, vmem_limit_bytes=24 << 20),
         cost_estimate=pl.CostEstimate(flops=16 << 30, bytes_accessed=24 << 20, transcendentals=0),
@@ -266,15 +269,17 @@
         finish_kernel,
         name="finish",
         out_shape=[
-            jax.ShapeDtypeStruct((1, NAUX, BS, NOCC), bf16),
-            jax.ShapeDtypeStruct((1, BS, BS), f32),
+            pltpu.HBM((1, NAUX, BS, NOCC), bf16),
+            pltpu.HBM((1, BS, BS), f32),
         ],
         in_specs=[vmem] * 5,
-        out_specs=[hbm, vmem],
+        out_specs=[hbm, hbm],
         scratch_shapes=[
             pltpu.VMEM((2 * len(LATE) * BS, DEPTH), bf16),
             pltpu.VMEM((2 * len(LATE), BS, NOCC), bf16),
+            pltpu.VMEM((1, BS, BS), f32),
             dma((NAUX,)),
+            dma(()),
         ],
         compiler_params=pltpu.CompilerParams(vmem_limit_bytes=24 << 20),
         cost_estimate=pl.CostEstimate(flops=2 << 30, bytes_accessed=16 << 20, transcendentals=0),

time: 107 us -> 106 us (level)
  no operation moved by 1% of the time
where the time goes in v3:
time: 106 us; the launch traced here: 105 us
  Pallas kernels  105 us (99%)
    pallas_call x1, Pallas kernels, shards(): pl.pallas_call(gather_kernel, name='gather', out_shape=[pltpu.VMEM((NAUX,...  98.8 us
    pallas_call x1, Pallas kernels, shards(): pl.pallas_call(finish_kernel, name='finish', out_shape=[pltpu.HBM((1, NAU...  5.9 us

profile of v3, /device:TPU:0, one launch (start us, length us, event | category | flops | bytes accessed | tf_op | source)
XLA Modules:
  0.0 105.4 jit_solution(4468757590776230132)
XLA Ops:
  0.6 98.8 %gather.1 = (bf16[32,128,1920]{2,1,0:T(8,128)(2,1)S(1)}, bf16[2,4,4,8,128,128]{5,4,3,2,1,0:T(8,128)(2,1)S(1)}, bf16[1024,1920]{1,0:T(8,128)(2,1)S(1)}, f32[16,1024]{1,0:T(8,128)S(1)}, f32[128,128]{1,0:T(8,128)S(1)}) custom-call(bf16[2,4,4,8,128,128]{5,4,3,2,1,0:T(8,128)(2,1)} %bitcast.2, bf16[1,128,1920]{2,1,0:T(8,128)(2,1)} %panel.1, ...), custom_call_target="tpu_custom_call" | custom-call | flops 17179869184 | bytes 25165824 | tf_op jit(solution)/shard_map/gather/pallas_call | solution.py:237
  99.5 5.9 %finish.1 = (bf16[1,32,128,1920]{3,2,1,0:T(8,128)(2,1)}, f32[1,128,128]{2,1,0:T(8,128)}) custom-call(bf16[32,128,1920]{2,1,0:T(8,128)(2,1)S(1)} %get-tuple-element.7.hv, bf16[2,4,4,8,128,128]{5,4,3,2,1,0:T(8,128)(2,1)S(1)} %get-tuple-element.8.fin, bf16[1024,1920]{1,0:T(8,128)(2,1)S(1)} %get-tuple-element.9.dens, f32[16,1024]{1,0:T(8,128)S(1)} %get-tuple-element.10.mask, ...), custom_call_target="tpu_custom_call" | custom-call | flops 2147483648 | bytes 16777216 | tf_op jit(solution)/shard_map/finish/pallas_call | solution.py:268

commit v4 on v3

--- a/solution.py
+++ b/solution.py
@@ -17,10 +17,12 @@
 DEPTH = NLB * BS
 SIDE = 4
 SCALE = 1.0 / (NAUX * NOCC)
+SENDS = (1, 3, 2)
 ORDER = (2, 3, 1)
+TURNS = (2, 3, 1)
 STEP = 640
 COLUMNS = ((0, 512), (512, 512), (1024, 512), (1536, 384))
-PAIRS = [(d, 0) for d in (0,) + ORDER] + [(d, e) for d in (0,) + ORDER for e in ORDER]
+PAIRS = [(d, 0) for d in (0,) + ORDER] + [(d, e) for d in (0,) + ORDER for e in TURNS]
 EARLY, LATE = PAIRS[:14], PAIRS[14:]
 
 
@@ -71,7 +73,7 @@
     pl.semaphore_wait(barrier, 10)
 
     relay_a, relay_b = {}, {}
-    for d in ORDER:
+    for d in SENDS:
         relay_a[d] = send(ints.at[0, (x + d) % SIDE], xa.at[d - 1], s_one.at[0, d], r_one.at[0, d], at_xz(d, 0))
         relay_b[d] = send(ints.at[1, :, (z + d) % SIDE], zb.at[d - 1], s_one.at[1, d], r_one.at[1, d], at_xz(0, d))
         relay_a[d].start()
@@ -80,7 +82,7 @@
     for d in ORDER:
         panels[d].start()
     direct = []
-    for e in ORDER:
+    for e in TURNS:
         direct.append(send(ints.at[0, x, (z + e) % SIDE], fin.at[0, 0, e], s_two.at[0, 0, e], r_fin.at[0, 0, e], at_xz(0, e)))
         direct.append(send(ints.at[1, (x + e) % SIDE, z], fin.at[1, e, 0], s_two.at[1, 0, e], r_fin.at[1, 0, e], at_xz(e, 0)))
     for copy in direct:
@@ -117,7 +119,7 @@
     for d in ORDER:
         relay_a[d].wait_recv()
         relay_b[d].wait_recv()
-        for e in ORDER:
+        for e in TURNS:
             second[0, d, e] = send(xa.at[d - 1, (z + e) % SIDE], fin.at[0, d, e], s_two.at[0, d, e], r_fin.at[0, d, e], at_xz(0, e))
             second[1, d, e] = send(zb.at[d - 1, (x + e) % SIDE], fin.at[1, e, d], s_two.at[1, d, e], r_fin.at[1, d, e], at_xz(e, 0))
             second[0, d, e].start()
@@ -162,19 +164,23 @@
         return 0
 
     lax.fori_loop(0, len(EARLY), step, 0)
+    for copy in list(relay_a.values()) + list(relay_b.values()) + direct + list(second.values()) + list(panels.values()) + list(shared.values()):
+        copy.wait_send()
     for d, e in LATE:
         pair(d, e)
-    for copy in list(relay_a.values()) + list(relay_b.values()) + direct + list(second.values()) + list(panels.values()) + list(shared.values()):
-        copy.wait_send()
 
 
 def pair_at(g):
-    def turn(i):
-        return (2 * i - i // 2) % SIDE
-
     h = lax.max(g - SIDE, 0)
     first = g < SIDE
-    return jnp.where(first, turn(g), turn(h // 3)), jnp.where(first, 0, turn(h % 3 + 1))
+    return pick(jnp.where(first, g, h // 3), (0,) + ORDER), jnp.where(first, 0, pick(h % 3, TURNS))
+
+
+def pick(i, values):
+    result = values[-1]
+    for k in range(len(values) - 2, -1, -1):
+        result = jnp.where(i == k, values[k], result)
+    return result
 
 
 def finish_kernel(hv, fin, dens, mask, kacc, halves, kblocks, lhs, late, kout, sems, k_sem):
@@ -200,7 +206,7 @@
         out(hv.at[pl.ds(spot, count)], spot, count)
 
     def unit(k):
-        d, e, p = 1, 3 - k // 2 * 2, k % 2
+        d, e, p = pick(k // 2, [pair[0] for pair in LATE]), pick(k // 2, [pair[1] for pair in LATE]), k % 2
         return p, (1 - p) * d + p * e, (1 - p) * e + p * d
 
     def stage(k, _):

time: 106 us -> 106 us (level)
  no operation moved by 1% of the time
where the time goes in v4:
time: 106 us; the launch traced here: 105 us
  Pallas kernels  105 us (99%)
    pallas_call x1, Pallas kernels, shards(): pl.pallas_call(gather_kernel, name='gather', out_shape=[pltpu.VMEM((NAUX,...  99 us
    pallas_call x1, Pallas kernels, shards(): pl.pallas_call(finish_kernel, name='finish', out_shape=[pltpu.HBM((1, NAU...  5.9 us

profile of v4, /device:TPU:0, one launch (start us, length us, event | category | flops | bytes accessed | tf_op | source)
XLA Modules:
  0.0 105.5 jit_solution(9858893648741797066)
XLA Ops:
  0.6 99.0 %gather.1 = (bf16[32,128,1920]{2,1,0:T(8,128)(2,1)S(1)}, bf16[2,4,4,8,128,128]{5,4,3,2,1,0:T(8,128)(2,1)S(1)}, bf16[1024,1920]{1,0:T(8,128)(2,1)S(1)}, f32[16,1024]{1,0:T(8,128)S(1)}, f32[128,128]{1,0:T(8,128)S(1)}) custom-call(bf16[2,4,4,8,128,128]{5,4,3,2,1,0:T(8,128)(2,1)} %bitcast.2, bf16[1,128,1920]{2,1,0:T(8,128)(2,1)} %panel.1, ...), custom_call_target="tpu_custom_call" | custom-call | flops 17179869184 | bytes 25165824 | tf_op jit(solution)/shard_map/gather/pallas_call | solution.py:243
  99.6 5.9 %finish.1 = (bf16[1,32,128,1920]{3,2,1,0:T(8,128)(2,1)}, f32[1,128,128]{2,1,0:T(8,128)}) custom-call(bf16[32,128,1920]{2,1,0:T(8,128)(2,1)S(1)} %get-tuple-element.7.hv, bf16[2,4,4,8,128,128]{5,4,3,2,1,0:T(8,128)(2,1)S(1)} %get-tuple-element.8.fin, bf16[1024,1920]{1,0:T(8,128)(2,1)S(1)} %get-tuple-element.9.dens, f32[16,1024]{1,0:T(8,128)S(1)} %get-tuple-element.10.mask, ...), custom_call_target="tpu_custom_call" | custom-call | flops 2147483648 | bytes 16777216 | tf_op jit(solution)/shard_map/finish/pallas_call | solution.py:274

commit v5 on v4

--- a/solution.py
+++ b/solution.py
@@ -74,17 +74,17 @@
 
     relay_a, relay_b = {}, {}
     for d in SENDS:
-        relay_a[d] = send(ints.at[0, (x + d) % SIDE], xa.at[d - 1], s_one.at[0, d], r_one.at[0, d], at_xz(d, 0))
-        relay_b[d] = send(ints.at[1, :, (z + d) % SIDE], zb.at[d - 1], s_one.at[1, d], r_one.at[1, d], at_xz(0, d))
+        relay_a[d] = send(ints.at[0, (x + d) % SIDE], xa.at[d - 1], s_one.at[0], r_one.at[0, d - 1], at_xz(d, 0))
+        relay_b[d] = send(ints.at[1, :, (z + d) % SIDE], zb.at[d - 1], s_one.at[1], r_one.at[1, d - 1], at_xz(0, d))
         relay_a[d].start()
         relay_b[d].start()
-    panels = {d: send(panel.at[0], prcv.at[o], s_pan.at[0, d], r_pan.at[0, d], at_orb(d, 0)) for d in ORDER}
+    panels = {d: send(panel.at[0], prcv.at[o], s_pan.at[0], r_pan.at[0, d], at_orb(d, 0)) for d in ORDER}
     for d in ORDER:
         panels[d].start()
     direct = []
     for e in TURNS:
-        direct.append(send(ints.at[0, x, (z + e) % SIDE], fin.at[0, 0, e], s_two.at[0, 0, e], r_fin.at[0, 0, e], at_xz(0, e)))
-        direct.append(send(ints.at[1, (x + e) % SIDE, z], fin.at[1, e, 0], s_two.at[1, 0, e], r_fin.at[1, 0, e], at_xz(e, 0)))
+        direct.append(send(ints.at[0, x, (z + e) % SIDE], fin.at[0, 0, e], s_two.at[0], r_fin.at[0, 0, e - 1], at_xz(0, e)))
+        direct.append(send(ints.at[1, (x + e) % SIDE, z], fin.at[1, e, 0], s_two.at[1], r_fin.at[1, 0, e - 1], at_xz(e, 0)))
     for copy in direct:
         copy.start()
     mine = [
@@ -99,7 +99,7 @@
     owners.start()
     for copy in mine:
         copy.start()
-    shared = {0: send(panel.at[0], prcv.at[o], s_pan.at[1, 0], r_pan.at[1, 0], at_orb(0, 1))}
+    shared = {0: send(panel.at[0], prcv.at[o], s_pan.at[1], r_pan.at[1, 0], at_orb(0, 1))}
     shared[0].start()
 
     masks.wait()
@@ -112,7 +112,7 @@
     for d in ORDER:
         panels[d].wait_recv()
         slot = (y + SIDE - d) % SIDE * 2 + c
-        shared[d] = send(prcv.at[slot], prcv.at[slot], s_pan.at[1, d], r_pan.at[1, d], at_orb(0, 1))
+        shared[d] = send(prcv.at[slot], prcv.at[slot], s_pan.at[1], r_pan.at[1, d], at_orb(0, 1))
         shared[d].start()
 
     second = {}
@@ -120,12 +120,12 @@
         relay_a[d].wait_recv()
         relay_b[d].wait_recv()
         for e in TURNS:
-            second[0, d, e] = send(xa.at[d - 1, (z + e) % SIDE], fin.at[0, d, e], s_two.at[0, d, e], r_fin.at[0, d, e], at_xz(0, e))
-            second[1, d, e] = send(zb.at[d - 1, (x + e) % SIDE], fin.at[1, e, d], s_two.at[1, d, e], r_fin.at[1, d, e], at_xz(e, 0))
+            second[0, d, e] = send(xa.at[d - 1, (z + e) % SIDE], fin.at[0, d, e], s_two.at[0], r_fin.at[0, d, e - 1], at_xz(0, e))
+            second[1, d, e] = send(zb.at[d - 1, (x + e) % SIDE], fin.at[1, e, d], s_two.at[1], r_fin.at[1, d, e - 1], at_xz(e, 0))
             second[0, d, e].start()
             second[1, d, e].start()
-        mine.append(pltpu.make_async_copy(xa.at[d - 1, z], fin.at[0, d, 0], d_sem.at[0, d]))
-        mine.append(pltpu.make_async_copy(zb.at[d - 1, x], fin.at[1, 0, d], d_sem.at[1, d]))
+        mine.append(pltpu.make_async_copy(xa.at[d - 1, z], fin.at[0, d, 0], d_sem.at[0, d - 1]))
+        mine.append(pltpu.make_async_copy(zb.at[d - 1, x], fin.at[1, 0, d], d_sem.at[1, d - 1]))
         mine[-2].start()
         mine[-1].start()
 
@@ -139,7 +139,7 @@
 
     def pair(d, e):
         for p, (dx, dz) in ((0, (d, e)), (1, (e, d))):
-            send(fin.at[p, dx, dz], fin.at[p, dx, dz], s_one.at[0, 0], r_fin.at[p, d, e], at_xz(1, 0)).wait_recv()
+            send(fin.at[p, dx, dz], fin.at[p, dx, dz], s_one.at[0], r_fin.at[p, d, e - 1], at_xz(1, 0)).wait_recv()
 
     def work(d, e):
         spots = [tile_of(x, z, d, e) * 2, tile_of(x, z, e, d) * 2 + 1]
@@ -164,8 +164,11 @@
         return 0
 
     lax.fori_loop(0, len(EARLY), step, 0)
-    for copy in list(relay_a.values()) + list(relay_b.values()) + direct + list(second.values()) + list(panels.values()) + list(shared.values()):
-        copy.wait_send()
+    for whole, sem in (
+        (xa, s_one.at[0]), (zb, s_one.at[1]), (xa, s_two.at[0]), (zb, s_two.at[1]),
+        (prcv.at[pl.ds(0, 3)], s_pan.at[0]), (prcv.at[pl.ds(0, 4)], s_pan.at[1]),
+    ):
+        send(whole, whole, sem, r_fin.at[0, 0, 0], at_xz(1, 0)).wait_send()
     for d, e in LATE:
         pair(d, e)
 
@@ -183,13 +186,10 @@
     return result
 
 
-def finish_kernel(hv, fin, dens, mask, kacc, halves, kblocks, lhs, late, kout, sems, k_sem):
+def finish_kernel(hv, fin, dens, mask, kacc, halves, kblocks, lhs, late, kout, sem, k_sem):
     x, z, y, c = place()
-    copies = []
-
     def out(source, spot, count):
-        copies.append(pltpu.make_async_copy(source, halves.at[0, pl.ds(spot, count)], sems.at[len(copies)]))
-        copies[-1].start()
+        pltpu.make_async_copy(source, halves.at[0, pl.ds(spot, count)], sem).start()
 
     left = [unit for d, e in LATE for unit in ((0, d, e), (1, e, d))]
     whole = [dx for dx in range(SIDE) if all(dx != unit[1] for unit in left)]
@@ -227,10 +227,10 @@
         out(late.at[pl.ds(k, 1)], tile_of(x, z, dx, dz) * 2 + p, 1)
     total = lax.fori_loop(0, len(left), lambda k, total: total + gram(late[k]), kacc[...])
     kout[0] = total * SCALE
-    copies.append(pltpu.make_async_copy(kout, kblocks, k_sem))
-    copies[-1].start()
-    for copy in copies:
-        copy.wait()
+    last = pltpu.make_async_copy(kout, kblocks, k_sem)
+    last.start()
+    pltpu.make_async_copy(hv, halves.at[0], sem).wait()
+    last.wait()
 
 
 def shards(integrals, panels, screen, owner_map):
@@ -259,14 +259,14 @@
             pltpu.VMEM((NAT, NLB, NRB), jnp.int32),
             pltpu.SMEM((NLB,), jnp.int32),
             pltpu.VMEM((2 * BS, DEPTH), bf16),
-            dma((2, 4)),
-            dma((2, 4)),
-            dma((2, 4, 4)),
-            dma((2, 4, 4)),
-            dma((2, 4)),
+            dma((2,)),
+            dma((2, 3)),
+            dma((2,)),
+            dma((2, 4, 3)),
+            dma((2,)),
             dma((2, 4)),
             dma((5,)),
-            dma((2, 4)),
+            dma((2, 3)),
         ],
         compiler_params=pltpu.CompilerParams(collective_id=0, has_side_effects=True, vmem_limit_bytes=24 << 20),
         cost_estimate=pl.CostEstimate(flops=16 << 30, bytes_accessed=24 << 20, transcendentals=0),
@@ -284,7 +284,7 @@
             pltpu.VMEM((2 * len(LATE) * BS, DEPTH), bf16),
             pltpu.VMEM((2 * len(LATE), BS, NOCC), bf16),
             pltpu.VMEM((1, BS, BS), f32),
-            dma((NAUX,)),
+            dma(()),
             dma(()),
         ],
         compiler_params=pltpu.CompilerParams(vmem_limit_bytes=24 << 20),

time: 106 us -> 105 us (level)
  no operation moved by 1% of the time
where the time goes in v5:
time: 105 us
  Pallas kernels  104 us (99%)
    pallas_call x1, Pallas kernels, shards(): pl.pallas_call(gather_kernel, name='gather', out_shape=[pltpu.VMEM((NAUX,...  98.5 us
    pallas_call x1, Pallas kernels, shards(): pl.pallas_call(finish_kernel, name='finish', out_shape=[pltpu.HBM((1, NAU...  5.62 us

profile of v5, /device:TPU:0, one launch (start us, length us, event | category | flops | bytes accessed | tf_op | source)
XLA Modules:
  0.0 104.7 jit_solution(18249508203499727297)
XLA Ops:
  0.6 98.5 %gather.1 = (bf16[32,128,1920]{2,1,0:T(8,128)(2,1)S(1)}, bf16[2,4,4,8,128,128]{5,4,3,2,1,0:T(8,128)(2,1)S(1)}, bf16[1024,1920]{1,0:T(8,128)(2,1)S(1)}, f32[16,1024]{1,0:T(8,128)S(1)}, f32[128,128]{1,0:T(8,128)S(1)}) custom-call(bf16[2,4,4,8,128,128]{5,4,3,2,1,0:T(8,128)(2,1)} %bitcast.2, bf16[1,128,1920]{2,1,0:T(8,128)(2,1)} %panel.1, ...), custom_call_target="tpu_custom_call" | custom-call | flops 17179869184 | bytes 25165824 | tf_op jit(solution)/shard_map/gather/pallas_call | solution.py:243
  99.1 5.6 %finish.1 = (bf16[1,32,128,1920]{3,2,1,0:T(8,128)(2,1)}, f32[1,128,128]{2,1,0:T(8,128)}) custom-call(bf16[32,128,1920]{2,1,0:T(8,128)(2,1)S(1)} %get-tuple-element.7.hv, bf16[2,4,4,8,128,128]{5,4,3,2,1,0:T(8,128)(2,1)S(1)} %get-tuple-element.8.fin, bf16[1024,1920]{1,0:T(8,128)(2,1)S(1)} %get-tuple-element.9.dens, f32[16,1024]{1,0:T(8,128)S(1)} %get-tuple-element.10.mask, ...), custom_call_target="tpu_custom_call" | custom-call | flops 2147483648 | bytes 16777216 | tf_op jit(solution)/shard_map/finish/pallas_call | solution.py:274

commit v6 on v5

--- a/solution.py
+++ b/solution.py
@@ -83,8 +83,8 @@
         panels[d].start()
     direct = []
     for e in TURNS:
-        direct.append(send(ints.at[0, x, (z + e) % SIDE], fin.at[0, 0, e], s_two.at[0], r_fin.at[0, 0, e - 1], at_xz(0, e)))
-        direct.append(send(ints.at[1, (x + e) % SIDE, z], fin.at[1, e, 0], s_two.at[1], r_fin.at[1, 0, e - 1], at_xz(e, 0)))
+        direct.append(send(ints.at[0, x, (z + e) % SIDE], fin.at[0, 0, e], s_two.at[0], r_fin.at[0, e - 1], at_xz(0, e)))
+        direct.append(send(ints.at[1, (x + e) % SIDE, z], fin.at[1, e, 0], s_two.at[1], r_fin.at[0, e - 1], at_xz(e, 0)))
     for copy in direct:
         copy.start()
     mine = [
@@ -120,8 +120,8 @@
         relay_a[d].wait_recv()
         relay_b[d].wait_recv()
         for e in TURNS:
-            second[0, d, e] = send(xa.at[d - 1, (z + e) % SIDE], fin.at[0, d, e], s_two.at[0], r_fin.at[0, d, e - 1], at_xz(0, e))
-            second[1, d, e] = send(zb.at[d - 1, (x + e) % SIDE], fin.at[1, e, d], s_two.at[1], r_fin.at[1, d, e - 1], at_xz(e, 0))
+            second[0, d, e] = send(xa.at[d - 1, (z + e) % SIDE], fin.at[0, d, e], s_two.at[0], r_fin.at[d, e - 1], at_xz(0, e))
+            second[1, d, e] = send(zb.at[d - 1, (x + e) % SIDE], fin.at[1, e, d], s_two.at[1], r_fin.at[d, e - 1], at_xz(e, 0))
             second[0, d, e].start()
             second[1, d, e].start()
         mine.append(pltpu.make_async_copy(xa.at[d - 1, z], fin.at[0, d, 0], d_sem.at[0, d - 1]))
@@ -138,8 +138,8 @@
         dens[j * BS : (j + 1) * BS, :] = prcv[own[j]]
 
     def pair(d, e):
-        for p, (dx, dz) in ((0, (d, e)), (1, (e, d))):
-            send(fin.at[p, dx, dz], fin.at[p, dx, dz], s_one.at[0], r_fin.at[p, d, e - 1], at_xz(1, 0)).wait_recv()
+        both = fin.at[0, pl.ds(0, 2), 0]
+        send(both, both, s_one.at[0], r_fin.at[d, e - 1], at_xz(1, 0)).wait_recv()
 
     def work(d, e):
         spots = [tile_of(x, z, d, e) * 2, tile_of(x, z, e, d) * 2 + 1]
@@ -168,7 +168,7 @@
         (xa, s_one.at[0]), (zb, s_one.at[1]), (xa, s_two.at[0]), (zb, s_two.at[1]),
         (prcv.at[pl.ds(0, 3)], s_pan.at[0]), (prcv.at[pl.ds(0, 4)], s_pan.at[1]),
     ):
-        send(whole, whole, sem, r_fin.at[0, 0, 0], at_xz(1, 0)).wait_send()
+        send(whole, whole, sem, r_fin.at[0, 0], at_xz(1, 0)).wait_send()
     for d, e in LATE:
         pair(d, e)
 
@@ -262,7 +262,7 @@
             dma((2,)),
             dma((2, 3)),
             dma((2,)),
-            dma((2, 4, 3)),
+            dma((4, 3)),
             dma((2,)),
             dma((2, 4)),
             dma((5,)),

time: 105 us -> 105 us (level)
  no operation moved by 1% of the time
where the time goes in v6:
time: 105 us
  Pallas kernels  104 us (99%)
    pallas_call x1, Pallas kernels, shards(): pl.pallas_call(gather_kernel, name='gather', out_shape=[pltpu.VMEM((NAUX,...  98.4 us
    pallas_call x1, Pallas kernels, shards(): pl.pallas_call(finish_kernel, name='finish', out_shape=[pltpu.HBM((1, NAU...  5.62 us

profile of v6, /device:TPU:0, one launch (start us, length us, event | category | flops | bytes accessed | tf_op | source)
XLA Modules:
  0.0 104.6 jit_solution(7361941990574444335)
XLA Ops:
  0.6 98.4 %gather.1 = (bf16[32,128,1920]{2,1,0:T(8,128)(2,1)S(1)}, bf16[2,4,4,8,128,128]{5,4,3,2,1,0:T(8,128)(2,1)S(1)}, bf16[1024,1920]{1,0:T(8,128)(2,1)S(1)}, f32[16,1024]{1,0:T(8,128)S(1)}, f32[128,128]{1,0:T(8,128)S(1)}) custom-call(bf16[2,4,4,8,128,128]{5,4,3,2,1,0:T(8,128)(2,1)} %bitcast.2, bf16[1,128,1920]{2,1,0:T(8,128)(2,1)} %panel.1, ...), custom_call_target="tpu_custom_call" | custom-call | flops 17179869184 | bytes 25165824 | tf_op jit(solution)/shard_map/gather/pallas_call | solution.py:243
  99.0 5.6 %finish.1 = (bf16[1,32,128,1920]{3,2,1,0:T(8,128)(2,1)}, f32[1,128,128]{2,1,0:T(8,128)}) custom-call(bf16[32,128,1920]{2,1,0:T(8,128)(2,1)S(1)} %get-tuple-element.7.hv, bf16[2,4,4,8,128,128]{5,4,3,2,1,0:T(8,128)(2,1)S(1)} %get-tuple-element.8.fin, bf16[1024,1920]{1,0:T(8,128)(2,1)S(1)} %get-tuple-element.9.dens, f32[16,1024]{1,0:T(8,128)S(1)} %get-tuple-element.10.mask, ...), custom_call_target="tpu_custom_call" | custom-call | flops 2147483648 | bytes 16777216 | tf_op jit(solution)/shard_map/finish/pallas_call | solution.py:274
